TPU v7x, 32 devices: a whole 2x2x4 slice. The times are simulated.
32 devices in a mesh: patch: 8 (over y, x, core), mlp: 4 (over z).
Axes of the slice: x: 2, y: 2, z: 4, core: 2. Of those that a mesh axis runs over, the one named last changes fastest.
Arguments:
- latent: bfloat16 [2048, 2432], P('patch', 'mlp'), may hold values from -24 to 24
- split_list: int32 [8, 4], P('patch'), may hold values from 0 to 256, as said below
- modulation: float32 [1, 6, 2432], replicated, may hold values from -3 to 3
- w_qkv: bfloat16 [2432, 3, 1536], P(None, None, 'mlp'), may hold values from -0.125 to 0.125
- w_out: bfloat16 [1536, 2432], P('mlp'), may hold values from -0.15625 to 0.15625
- w_up: bfloat16 [2432, 5120], P(None, 'mlp'), may hold values from -0.125 to 0.125
- w_down: bfloat16 [5120, 2432], P('mlp'), may hold values from -0.078125 to 0.078125
- qk_gains: float32 [3, 64], replicated, may hold values from 1.6 to 2.4
- text_kv: bfloat16 [2, 1, 154, 1536], P(None, None, None, 'mlp'), may hold values from -6 to 6
- timestep: int32 [1], replicated, may hold values from 0 to 27
- step_sizes: float32 [28], replicated, may hold values from -0.6 to -0.1
Outputs:
- latent_next: bfloat16 [2048, 2432], P('patch', 'mlp')
Inputs may be any that keep to these rules, and one draw needn't show every extreme that they name: `split_list`: row d holds device d's tile pieces (item, count, item, count); over all devices the counts of every item add up to 1024. A device's two counts add up to at most 256, to exactly 256 on some device and to 0 on another. The devices holding an item's tokens form a run of consecutive indices of patch, taken cyclically. Both pieces may name the same item; they are then two parts of it.
All inputs are finite; a program needn't handle non-finite values.
Results may differ from a plain program's by a relative error of at most 0.0049.
Values may be sent and summed in bfloat16 or wider, within the bound.
A program may use at most 128 MiB of HBM per device.

v0:
```python
import jax
import jax.numpy as jnp
from jax import lax
from jax.sharding import PartitionSpec as P

HEAD = 64


norm_eps = 1e-06
block_rows = 512


def layer_norm(row_data):
    row_mean = jnp.mean(row_data, axis=-1, keepdims=True)
    centred = row_data - row_mean
    variance = jnp.mean(centred * centred, axis=-1, keepdims=True)
    return centred * lax.rsqrt(variance + norm_eps)


def head_norm(row_data, gain_row):
    shaped = row_data.reshape(row_data.shape[0], -1, HEAD)
    mean_square = jnp.mean(shaped * shaped, axis=-1, keepdims=True)
    return (shaped * lax.rsqrt(mean_square + norm_eps) * gain_row).reshape(row_data.shape)


def attend_dense(state_pair, queries, query_tags, key_rows, value_rows, key_tags):
    numerator, denominator = state_pair
    query_count = queries.shape[0]
    heads_here = queries.shape[1] // HEAD
    query_heads = queries.reshape(query_count, heads_here, HEAD)
    key_heads = key_rows.reshape(key_rows.shape[0], heads_here, HEAD)
    value_heads = value_rows.reshape(value_rows.shape[0], heads_here, HEAD)
    scores = jnp.einsum(
        "qhd,khd->qhk", query_heads, key_heads, preferred_element_type=jnp.float32
    ) * HEAD ** (-0.5)
    same_item = (query_tags[:, None] == key_tags[None, :])[:, None, :]
    weights = jnp.where(same_item, jnp.exp(scores), 0.0)
    denominator = denominator + jnp.sum(weights, axis=-1)
    numerator = numerator + jnp.einsum(
        "qhk,khd->qhd",
        weights.astype(jnp.bfloat16),
        value_heads,
        preferred_element_type=jnp.float32,
    )
    return (numerator, denominator)


def attend_block(state_pair, queries, query_tags, key_rows, value_rows, key_tags):
    touching = jnp.any(query_tags[:, None] == key_tags[None, :])

    def work(inner):
        return attend_dense(inner, queries, query_tags, key_rows, value_rows, key_tags)

    def skip(inner):
        return inner

    return lax.cond(touching, work, skip, state_pair)


def attend(state_pair, queries, query_tags, key_rows, value_rows, key_tags):
    key_count = key_rows.shape[0]
    if key_count > 2 * block_rows and key_count % block_rows == 0:

        def one_block(block_index, inner):
            offset = block_index * block_rows
            return attend_block(
                inner,
                queries,
                query_tags,
                lax.dynamic_slice_in_dim(key_rows, offset, block_rows, 0),
                lax.dynamic_slice_in_dim(value_rows, offset, block_rows, 0),
                lax.dynamic_slice_in_dim(key_tags, offset, block_rows, 0),
            )

        return lax.fori_loop(0, key_count // block_rows, one_block, state_pair)
    return attend_block(state_pair, queries, query_tags, key_rows, value_rows, key_tags)


def body(
    latent,
    split_list,
    modulation,
    w_qkv,
    w_out,
    w_up,
    w_down,
    qk_gains,
    text_kv,
    timestep,
    step_sizes,
):
    share_cols = latent.shape[1]
    row_data = lax.all_gather(latent, "mlp", axis=1, tiled=True)
    capacity = row_data.shape[0]
    item_total = modulation.shape[0]
    item_a = split_list[0, 0]
    count_a = split_list[0, 1]
    item_b = split_list[0, 2]
    count_b = split_list[0, 3]
    slot_ids = jnp.arange(capacity, dtype=jnp.int32)
    in_first = slot_ids < count_a
    slot_live = slot_ids < count_a + count_b
    slot_item = jnp.where(in_first, item_a, jnp.where(slot_live, item_b, -1))
    item_ids = jnp.arange(item_total, dtype=jnp.int32)
    one_hot = (slot_item[:, None] == item_ids[None, :]).astype(jnp.float32)
    slot_mods = jnp.dot(
        one_hot,
        modulation.reshape(item_total, -1),
        precision=lax.Precision.HIGHEST,
        preferred_element_type=jnp.float32,
    ).reshape(capacity, 6, -1)
    slot_step = jnp.dot(
        one_hot,
        jnp.take(step_sizes, timestep),
        precision=lax.Precision.HIGHEST,
        preferred_element_type=jnp.float32,
    )
    float_rows = row_data.astype(jnp.float32)
    normed_one = (layer_norm(float_rows) * (1.0 + slot_mods[:, 1]) + slot_mods[:, 0]).astype(
        jnp.bfloat16
    )
    projected = jnp.einsum("nd,dch->nch", normed_one, w_qkv, preferred_element_type=jnp.float32)
    queries = head_norm(projected[:, 0], qk_gains[0]).astype(jnp.bfloat16)
    key_rows = head_norm(projected[:, 1], qk_gains[1]).astype(jnp.bfloat16)
    value_rows = projected[:, 2].astype(jnp.bfloat16)
    head_cols = queries.shape[1]
    heads_here = head_cols // HEAD
    text_pair = jnp.take(text_kv, jnp.stack([item_a, item_b]), axis=1)
    text_keys = head_norm(
        text_pair[0].reshape(-1, head_cols).astype(jnp.float32), qk_gains[2]
    ).astype(jnp.bfloat16)
    text_values = text_pair[1].reshape(-1, head_cols)
    second_tag = jnp.where(item_b != item_a, item_b, -2)
    text_tags = jnp.repeat(jnp.stack([item_a, second_tag]), text_kv.shape[2]).astype(jnp.bfloat16)
    query_tags = slot_item.astype(jnp.bfloat16)
    key_tags = jnp.where(slot_live, slot_item, -3).astype(jnp.bfloat16)
    empty_state = (
        jnp.zeros((capacity, heads_here, HEAD), jnp.float32),
        jnp.zeros((capacity, heads_here), jnp.float32),
    )
    start_state = attend(empty_state, queries, query_tags, text_keys, text_values, text_tags)
    numerator, denominator = attend(
        start_state,
        queries,
        query_tags,
        lax.all_gather(key_rows, "patch", axis=0, tiled=True),
        lax.all_gather(value_rows, "patch", axis=0, tiled=True),
        lax.all_gather(key_tags, "patch", axis=0, tiled=True),
    )
    safe_denominator = denominator + (slot_item < 0).astype(jnp.float32)[:, None]
    attended = (
        (numerator / safe_denominator[:, :, None]).reshape(capacity, head_cols).astype(jnp.bfloat16)
    )
    head_part = jnp.dot(attended, w_out, preferred_element_type=jnp.float32)
    col_first = lax.axis_index("mlp") * share_cols
    attn_total = lax.psum(head_part, "mlp")
    after_attn = float_rows + slot_mods[:, 2] * attn_total
    normed_two = (layer_norm(after_attn) * (1.0 + slot_mods[:, 4]) + slot_mods[:, 3]).astype(
        jnp.bfloat16
    )
    up_total = jnp.dot(normed_two, w_up, preferred_element_type=jnp.float32)
    attn_share = lax.dynamic_slice_in_dim(after_attn, col_first, share_cols, 1)
    hidden_units = jax.nn.gelu(up_total, approximate=True).astype(jnp.bfloat16)
    unit_part = jnp.dot(hidden_units, w_down, preferred_element_type=jnp.float32)
    unit_total = lax.psum_scatter(unit_part, "mlp", scatter_dimension=1, tiled=True)
    gate_share = lax.dynamic_slice_in_dim(slot_mods[:, 5], col_first, share_cols, 1)
    after_mlp = attn_share + gate_share * unit_total
    next_rows = latent.astype(jnp.float32) + slot_step[:, None] * after_mlp
    return jnp.where(slot_live[:, None], next_rows, 0.0).astype(jnp.bfloat16)


def solution(mesh):
    return jax.shard_map(
        body,
        mesh=mesh,
        in_specs=(
            P("patch", "mlp"),
            P("patch", None),
            P(),
            P(None, None, "mlp"),
            P("mlp", None),
            P(None, "mlp"),
            P("mlp", None),
            P(),
            P(None, None, None, "mlp"),
            P(),
            P(),
        ),
        out_specs=P("patch", "mlp"),
        check_vma=False,
    )
```

profile of v0, /device:TPU:0, one launch (start us, length us, event | category | flops | bytes accessed | tf_op | source)
XLA Modules:
  0.0 319.1 jit_solution(8434744912893777445)
XLA Ops:
  13.5 1.9 broadcast_select_fusion.1
  15.4 6.1 %broadcast_multiply_fusion = f32[256,6,2432]{0,2,1:T(8,128)} fusion(f32[6,2432]{1,0:T(8,128)S(1)} %bitcast.153, f32[256]{0:T(256)S(1)} %get-tuple-element.424), kind=kLoop, calls=%fused_computation.23 | loop fusion | flops 3735552 | bytes 15001600 | tf_op jit(solution)/shard_map/dot_general | solution.py:106
  21.6 21.7 %all-gather.6.cloned.1.call-done = bf16[256,2432]{0,1:T(8,128)(2,1)} async-done(((bf16[256,608]{0,1:T(8,128)(2,1)}), bf16[256,2432]{0,1:T(8,128)(2,1)}) %all-gather.6.cloned.1.call-update) | async-done | bytes 1245200 | tf_op jit(solution)/shard_map/all_gather | solution.py:93
  46.7 6.0 %fusion.44 = f32[256,3,384]{2,0,1:T(8,128)S(1)} fusion(bf16[2432,3,384]{2,0,1:T(8,128)(2,1)} %param.20, f32[256,6,2432]{0,2,1:T(8,128)} %broadcast_multiply_fusion, bf16[256,2432]{0,1:T(8,128)(2,1)S(1)} %copy-done.2, f32[256]{0:T(256)S(1)} %add_rsqrt_fusion.4, f32[256]{0:T(256)S(1)} %broadcast_multiply_fusion.2), kind=kOutput, calls=%fused_computation.58 | convolution fusion | flops 1438810112 | bytes 13010944 | tf_op jit(solution)/shard_map/nd,dch->nch/dot_general | solution.py:122
  54.7 2.1 slice_multiply_fusion
  61.2 2.1 fusion.60
  75.1 2.6 reshape.303
  77.7 2.1 copy.113
  79.7 2.2 fusion.63
  81.9 2.6 mul.193
  86.5 2.1 copy.95
  88.7 9.0 %all-gather.1 = bf16[8,1,256]{2,1,0:T(2,128)(2,1)S(1)} all-gather(bf16[1,1,256]{2,1,0:T(2,128)(2,1)S(1)} %reshape.300), channel_id=1, replica_groups=mesh['patch'=8,'mlp'=4] {'patch'}, dimensions={0}, use_global_device_ids=true | all-gather | bytes 4608 | tf_op jit(solution)/shard_map/all_gather | solution.py:148
  100.5 8.4 %conditional.2 = (f32[256,6,64]{0,2,1:T(8,128)S(1)}, f32[256,6]{0,1:T(8,128)S(1)}) conditional(s32[]{:T(128)} %convert_element_type.111, () %tuple.38, (bf16[256]{0:T(256)(128)(2,1)S(1)}, s32[2]{0:T(128)S(1)}, bf16[308,384]{1,0:T(8,128)(2,1)}, bf16[256,384]{1,0:T(8,128)(2,1)S(1)}, bf16[2,2,154,384]{2,1,3,0:T(2,128)(2,1)}) %tuple.110), branch_computations={%region_5.6_spmd, %region_6.8_spmd} | conditional | flops 123080192 | bytes 5880796 | solution.py:57
  100.5 2.0 slice.38
  102.5 2.0 reshape_reshape_squeeze.2
  108.9 2.6 copy.105
  111.5 2.6 copy.103
  114.1 29.6 %while.17 = (s32[]{:T(128)}, f32[256,6,64]{0,2,1:T(8,128)S(1)}, f32[256,6]{0,1:T(8,128)S(1)}, bf16[2048]{0:T(1024)(128)(2,1)S(1)}, bf16[2048,384]{0,1:T(8,128)(2...) while((s32[]{:T(128)}, f32[256,6,64]{0,2,1:T(8,128)S(1)}, ...), condition=%wide.region_14.15_spmd.clone, body=%wide.region_9.14_spmd.clone.sunk | while | flops 206537984 | bytes 10057545 | solution.py:75
  117.6 3.9 %conditional.5 = ((f32[256,6,64]{0,2,1:T(8,128)S(1)}, f32[256,6]{0,1:T(8,128)S(1)})) conditional(s32[]{:T(128)} %convert_element_type.190, (f32[256,6,64]{0,2,1:T(8,128)S(1)}, f32[256,6]{0,1:T(8,128)S(1)}) %tuple.89, (bf16[256]{0:T(256)(128)(2,1)S(1)}, bf16[512]{0:T(512)(128)(2,1)S(1)}, bf16[2048,384]{0,1:T(8,128)(2,1)}, s32[]{:T(128)}, ...), branch_computations={%region_11.11_spmd, %region_12.13_spmd} | conditional | flops 206274560 | bytes 10053148 | solution.py:57
  121.6 1.9 fusion.89
  125.0 3.9 %conditional.5 = ((f32[256,6,64]{0,2,1:T(8,128)S(1)}, f32[256,6]{0,1:T(8,128)S(1)})) conditional(s32[]{:T(128)} %convert_element_type.190, (f32[256,6,64]{0,2,1:T(8,128)S(1)}, f32[256,6]{0,1:T(8,128)S(1)}) %tuple.89, (bf16[256]{0:T(256)(128)(2,1)S(1)}, bf16[512]{0:T(512)(128)(2,1)S(1)}, bf16[2048,384]{0,1:T(8,128)(2,1)}, s32[]{:T(128)}, ...), branch_computations={%region_11.11_spmd, %region_12.13_spmd} | conditional | flops 206274560 | bytes 10053148 | solution.py:57
  129.0 1.9 fusion.89
  132.4 3.9 %conditional.5 = ((f32[256,6,64]{0,2,1:T(8,128)S(1)}, f32[256,6]{0,1:T(8,128)S(1)})) conditional(s32[]{:T(128)} %convert_element_type.190, (f32[256,6,64]{0,2,1:T(8,128)S(1)}, f32[256,6]{0,1:T(8,128)S(1)}) %tuple.89, (bf16[256]{0:T(256)(128)(2,1)S(1)}, bf16[512]{0:T(512)(128)(2,1)S(1)}, bf16[2048,384]{0,1:T(8,128)(2,1)}, s32[]{:T(128)}, ...), branch_computations={%region_11.11_spmd, %region_12.13_spmd} | conditional | flops 206274560 | bytes 10053148 | solution.py:57
  136.4 1.9 fusion.89
  139.8 3.9 %conditional.5 = ((f32[256,6,64]{0,2,1:T(8,128)S(1)}, f32[256,6]{0,1:T(8,128)S(1)})) conditional(s32[]{:T(128)} %convert_element_type.190, (f32[256,6,64]{0,2,1:T(8,128)S(1)}, f32[256,6]{0,1:T(8,128)S(1)}) %tuple.89, (bf16[256]{0:T(256)(128)(2,1)S(1)}, bf16[512]{0:T(512)(128)(2,1)S(1)}, bf16[2048,384]{0,1:T(8,128)(2,1)}, s32[]{:T(128)}, ...), branch_computations={%region_11.11_spmd, %region_12.13_spmd} | conditional | flops 206274560 | bytes 10053148 | solution.py:57
  143.8 2.4 fusion.75
  146.3 98.0 %all-reduce.2.cloned.1.call-done = f32[256,2432]{0,1:T(8,128)} async-done(((f32[256,2432]{0,1:T(8,128)}), f32[256,2432]{0,1:T(8,128)}) %all-reduce.2.cloned.1.call-update) | async-done | bytes 2490384 | tf_op jit(solution)/shard_map/psum | solution.py:156
  244.3 2.9 fusion.71
  249.0 12.0 %convolution_bitcast_fusion.1 = f32[2432,256]{1,0:T(8,128)} fusion(bf16[1280,2432]{1,0:T(8,128)(2,1)} %param.23, bf16[2432,1280]{1,0:T(8,128)(2,1)} %param.22, f32[256,6,2432]{0,2,1:T(8,128)} %broadcast_multiply_fusion, f32[256,2432]{0,1:T(8,128)} %copy-done.1, f32[256]{0:T(256)S(1)} %add_rsqrt_fusion.3, f32[256]{0:T(256)S(1)} %broadcast_multiply_fusion.1), kind=kOutput, calls=%fused_computation.24 | convolution fusion | flops 3194355712 | bytes 22415360
  261.0 3.4 %slice.85 = f32[256,1,2432]{0,2,1:T(8,128)} slice(f32[256,6,2432]{0,2,1:T(8,128)} %broadcast_multiply_fusion), slice={[0:256], [5:6], [0:2432]} | slice | bytes 4980736 | tf_op jit(solution)/shard_map/slice | solution.py:166
  264.4 45.9 %reduce-scatter.4.cloned.1.call-done = f32[608,256]{1,0:T(8,128)} async-done(((f32[2432,256]{1,0:T(8,128)}), f32[608,256]{1,0:T(8,128)}) %reduce-scatter.4.cloned.1.call-update) | async-done | bytes 622608
  310.3 2.3 fusion.58
  (114 shorter events, 55.0 us)
Async XLA Ops:
  6.5 137.3 %copy-start = (bf16[384,2432]{1,0:T(8,128)(2,1)S(1)}, bf16[384,2432]{1,0:T(8,128)(2,1)}, u32[]{:S(2)}) copy-start(bf16[384,2432]{1,0:T(8,128)(2,1)} %param.21) | copy-start | bytes 5603332
  6.5 36.7 %all-gather.6.cloned.1.call-start = ((), (), s32[]{:S(2)}) async-start(), calls=%async_computation.1 | async-start | bytes 1556480 | tf_op jit(solution)/shard_map/all_gather | solution.py:93
  7.3 101.7 %all-gather.10.cloned.1.call-start = ((), (), s32[]{:S(2)}) async-start(), calls=%async_computation.4 | async-start | bytes 1769472 | tf_op jit(solution)/shard_map/all_gather | solution.py:147
  43.2 3.4 %copy-start.2 = (bf16[256,2432]{0,1:T(8,128)(2,1)S(1)}, bf16[256,2432]{0,1:T(8,128)(2,1)}, u32[]{:S(2)}) copy-start(bf16[256,2432]{0,1:T(8,128)(2,1)} %all-gather.6.cloned.1.call-done) | copy-start | bytes 3735556
  46.7 7.9 %copy-start.7 = (f32[3,64]{1,0:T(4,128)S(1)}, f32[3,64]{1,0:T(4,128)}, u32[]{:S(2)}) copy-start(f32[3,64]{1,0:T(4,128)} %param.24) | copy-start | bytes 2308
  52.7 1.0 copy-start.4
  54.5 57.1 %all-gather.8.cloned.1.call-start = ((), (), s32[]{:S(2)}) async-start(), calls=%async_computation.2 | async-start | bytes 1769472 | tf_op jit(solution)/shard_map/all_gather | solution.py:146
  63.3 181.0 %all-reduce.2.cloned.1.call-start = ((), (), s32[]{:S(2)}) async-start(), calls=%async_computation.3 | async-start | bytes 4980736 | tf_op jit(solution)/shard_map/psum | solution.py:156
  72.9 0.9 copy-start.3
  106.6 1.7 copy-start.6
  146.3 164.0 %reduce-scatter.4.cloned.1.call-start = ((), (), s32[]{:S(2)}) async-start(), calls=%async_computation.5 | async-start | bytes 3112960
  247.2 1.4 copy-start.1
  261.0 49.3 %copy-start.5 = (bf16[256,608]{0,1:T(8,128)(2,1)S(1)}, bf16[256,608]{0,1:T(8,128)(2,1)}, u32[]{:S(2)}) copy-start(bf16[256,608]{0,1:T(8,128)(2,1)} %param.17) | copy-start | bytes 933892
Sparse Core Ops, SparseCore 0:
  8.9 34.2 all-gather.5
  54.6 24.7 all-gather.9
  81.3 25.7 all-gather.7
  146.4 97.8 all-reduce.1
  261.1 49.0 reduce-scatter.3
where the time goes:
time: 321 us; the launch traced here: 319 us
  waiting for transfers between devices  166 us (52%)
  local copies, waits for them, and re-layouts  45.1 us (14%)
  other arithmetic  44.3 us (14%)
  matrix products  32.5 us (10%)
  between operations  18.6 us (6%)
  blocking collectives  9.01 us (3%)
    psum x1, waiting for transfers between devices, body(): attn_total = lax.psum(head_part, 'mlp')  98 us
    unnamed x6, waiting for transfers between devices  46.6 us
    all_gather x1, waiting for transfers between devices, body(): row_data = lax.all_gather(latent, 'mlp', axis=1, tiled=True)  21.7 us
    unnamed x1, matrix products  12 us
    unnamed x20, local copies, waits for them, and re-layouts  10.3 us
    all_gather x1, blocking collectives, body(): lax.all_gather(key_tags, 'patch', axis=0, tiled=True)  9.01 us
    dot_general x5, matrix products, attend_dense(): jnp.einsum('qhd,khd->qhk', query_heads, key_heads, preferred_element_type...  8.96 us
    convert_element_type x4, other arithmetic, body(): query_tags = slot_item.astype(jnp.bfloat16)  7.74 us
  transfers between devices with their start and end apart: 5, of which 3 were waited for; matrix products, arithmetic and copies ran while one was open for 18% of the time, Pallas kernels for 0%

commit v1 on v0

v1 whole, which is shorter than its diff:
```python
import functools

import jax
import jax.numpy as jnp
from jax import lax
from jax.experimental import pallas as pl
from jax.experimental.pallas import tpu as pltpu
from jax.sharding import PartitionSpec as P

HEAD = 64
IMG = 1024
norm_eps = 1e-06
MESH = pl.DeviceIdType.MESH
f32 = jnp.float32
bf16 = jnp.bfloat16


def layer_norm(rows):
    mean = jnp.mean(rows, axis=-1, keepdims=True)
    centred = rows - mean
    variance = jnp.mean(centred * centred, axis=-1, keepdims=True)
    return centred * lax.rsqrt(variance + norm_eps)


def head_norm(rows, gain):
    mean_square = jnp.mean(rows * rows, axis=0, keepdims=True)
    return rows * lax.rsqrt(mean_square + norm_eps) * gain


def column_chunks(width, step):
    start = 0
    while start < width:
        size = min(step, width - start)
        yield start, size
        start += size


def kernel(
    n, nz, txt,
    lat_ref, split_ref, mod_ref, gain_ref, text_ref, wq_hbm, wo_hbm, wu_hbm, wd_hbm,
    out_ref,
    wq, wo, wu, wd, split_all, t_ref, recv_a, m_ref, e_ref, sel, x_t, q_t, kv_t, q_all, kv_all,
    att_snd, att_t, part_t, recv_e, ga_t, mid_t, recv_g, fin_t, recv_f, res, recv_i,
    w_sem, send_sem, recv_sem,
):
    p = lax.axis_index("patch")
    m = lax.axis_index("mlp")
    share, cap = lat_ref.shape
    half = share // 2
    comp = sel.shape[2]
    width = x_t.shape[0]
    group = IMG // comp
    cols = q_t.shape[0]
    hcols = cols // 2
    heads_half = hcols // HEAD
    c = lax.rem(p, 2)
    pair = p // 2
    sib = p + 1 - 2 * c
    gbase = (p // group) * group
    gpos = p - gbase

    def al(value, unit):
        return pl.multiple_of(value, unit)

    weights = [(wq_hbm, wq), (wo_hbm, wo), (wu_hbm, wu), (wd_hbm, wd)]
    loads = [pltpu.make_async_copy(a, b, w_sem.at[i]) for i, (a, b) in enumerate(weights)]
    for load in loads:
        load.start()

    barrier = pltpu.get_barrier_semaphore()
    for o in range(1, n):
        pl.semaphore_signal(barrier, inc=1, device_id=(lax.rem(p + o, n), m), device_id_type=MESH)
    for o in range(1, nz):
        for q in (p, sib):
            pl.semaphore_signal(barrier, inc=1, device_id=(q, lax.rem(m + o, nz)), device_id_type=MESH)
    pl.semaphore_wait(barrier, n - 1 + 2 * (nz - 1))

    sends = []
    counter = [0]
    rbase = {}
    spot = 0
    for name, count in (
        ("split", n), ("a", n), ("b", 2 * nz), ("q", 1), ("kv", group), ("d", 1),
        ("e", nz), ("f", nz), ("g", nz), ("h", n), ("i", 1),
    ):
        rbase[name] = spot
        spot += count

    def push(src, dst, name, slot, device):
        copy = pltpu.make_async_remote_copy(
            src_ref=src, dst_ref=dst, send_sem=send_sem.at[counter[0]],
            recv_sem=recv_sem.at[rbase[name] + slot], device_id=device, device_id_type=MESH,
        )
        counter[0] += 1
        copy.start()
        sends.append(copy)

    def arrived(dst, name, slot):
        pltpu.make_async_remote_copy(
            src_ref=dst, dst_ref=dst, send_sem=send_sem.at[0],
            recv_sem=recv_sem.at[rbase[name] + slot], device_id=(sib, m), device_id_type=MESH,
        ).wait_recv()

    for o in range(1, n):
        d = lax.rem(p + o, n)
        push(split_ref, split_all.at[pl.ds(al(p * 8, 8), 8), :], "split", p, (d, m))
    for o in range(1, n):
        d = lax.rem(p + o, n)
        push(
            lat_ref.at[pl.ds(al(lax.rem(d, 2) * half, 16), half), :],
            recv_a.at[:, pl.ds(al(p * cap, 128), cap)], "a", p, (d, m),
        )
    split_all[pl.ds(al(p * 8, 8), 8), :] = split_ref[...]
    recv_a[:, pl.ds(al(p * cap, 128), cap)] = lat_ref[pl.ds(al(c * half, 16), half), :]
    for o in range(1, n):
        s = lax.rem(p + o, n)
        arrived(split_all.at[pl.ds(al(s * 8, 8), 8), :], "split", s)

    info = split_all[...]
    rows8 = info.shape[0]
    item_a, count_a = info[:, 0:1], info[:, 1:2]
    item_b, count_b = info[:, 2:3], info[:, 3:4]
    lane = lax.broadcasted_iota(jnp.int32, (rows8, 128), 1).astype(f32)
    held = jnp.where(item_a == lane, count_a, 0.0) + jnp.where(item_b == lane, count_b, 0.0)
    row_i = lax.broadcasted_iota(jnp.int32, (rows8, rows8), 0)
    row_k = lax.broadcasted_iota(jnp.int32, (rows8, rows8), 1)
    lower = jnp.where((row_k % 8 == 0) & (row_k // 8 < row_i // 8), 1.0, 0.0)
    before = jnp.dot(lower.astype(bf16), held.astype(bf16), preferred_element_type=f32)
    base_a = jnp.sum(jnp.where(item_a == lane, before, 0.0), axis=1, keepdims=True)
    base_b = jnp.sum(jnp.where(item_b == lane, before, 0.0), axis=1, keepdims=True)
    base_b = base_b + jnp.where(item_b == item_a, count_a, 0.0)
    slot = lax.broadcasted_iota(jnp.int32, (rows8, cap), 1).astype(f32)
    t_ref[...] = jnp.where(
        slot < count_a,
        item_a * IMG + base_a + slot,
        jnp.where(slot < count_a + count_b, item_b * IMG + base_b + slot - count_a, -1.0),
    )
    want = (lax.broadcasted_iota(jnp.int32, (2 * comp, cap), 0) + pair * (2 * comp)).astype(f32)
    for s in range(n):
        m_ref[:, s * cap:(s + 1) * cap] = jnp.where(
            t_ref[s * 8:s * 8 + 1, :] == want, 1.0, 0.0
        ).astype(bf16)
    for k in range(2):
        mine = t_ref[pl.ds(al((2 * pair + k) * 8, 8), 8), :][0:1, :]
        for s in range(n):
            rows = (lax.broadcasted_iota(jnp.int32, (comp, cap), 0) + s * comp).astype(f32)
            e_ref[s * comp:(s + 1) * comp, k * cap:(k + 1) * cap] = jnp.where(
                mine == rows, 1.0, 0.0
            ).astype(bf16)
    for o in range(1, n):
        s = lax.rem(p + o, n)
        arrived(recv_a.at[:, pl.ds(al(s * cap, 128), cap)], "a", s)
    chosen = lax.dot_general(
        recv_a[...], m_ref[...], (((1,), (1,)), ((), ())), preferred_element_type=f32
    ).astype(bf16)
    sel[0] = chosen[:, :comp]
    sel[1] = chosen[:, comp:]

    def x_rows(z, core):
        return pl.ds(al(z * share + core * half, 16), half)

    for o in range(1, nz):
        z = lax.rem(m + o, nz)
        for k in range(2):
            push(sel.at[k], x_t.at[x_rows(m, c), :], "b", 2 * m + c, (2 * pair + k, z))
    push(sel.at[1 - c], x_t.at[x_rows(m, c), :], "b", 2 * m + c, (sib, m))
    x_t[x_rows(m, c), :] = sel[c]
    arrived(x_t.at[x_rows(m, 1 - c), :], "b", 2 * m + 1 - c)
    for o in range(1, nz):
        z = lax.rem(m + o, nz)
        for k in range(2):
            arrived(x_t.at[x_rows(z, k), :], "b", 2 * z + k)
    x_all = x_t[...].astype(f32).T
    normed = (layer_norm(x_all) * (1.0 + mod_ref[1:2, :]) + mod_ref[0:1, :]).astype(bf16)
    loads[0].wait()
    for j, (gain_col, scale) in enumerate(((1, 1.0), (None, 1.0), (0, HEAD ** -0.5))):
        which = (1, 2, 0)[j]
        proj = jnp.dot(normed, wq[which], preferred_element_type=f32).T
        for h in range(cols // HEAD):
            rows = proj[h * HEAD:(h + 1) * HEAD]
            if gain_col is not None:
                rows = head_norm(rows, gain_ref[:, gain_col:gain_col + 1]) * scale
            if which == 0:
                q_t[h * HEAD:(h + 1) * HEAD, :] = rows.astype(bf16)
            else:
                kv_t[which - 1, h * HEAD:(h + 1) * HEAD, :] = rows.astype(bf16)
        if which == 2:
            for o in range(1, group):
                pos = lax.rem(gpos + o, group)
                push(
                    kv_t.at[:, pl.ds(al(lax.rem(pos, 2) * hcols, 16), hcols), :],
                    kv_all.at[:, :, pl.ds(al(gpos * comp, 128), comp)], "kv", gpos, (gbase + pos, m),
                )
            kv_all[:, :, pl.ds(al(gpos * comp, 128), comp)] = kv_t[:, pl.ds(al(c * hcols, 16), hcols), :]
    push(
        q_t.at[pl.ds(al((1 - c) * hcols, 16), hcols), :],
        q_all.at[:, pl.ds(al(c * comp, 128), comp)], "q", 0, (sib, m),
    )
    q_all[:, pl.ds(al(c * comp, 128), comp)] = q_t[pl.ds(al(c * hcols, 16), hcols), :]

    text_pad = text_ref.shape[2]
    text_k = text_ref[0, pl.ds(al(c * hcols, 16), hcols), :].astype(f32)
    text_v = text_ref[1, pl.ds(al(c * hcols, 16), hcols), :]
    arrived(q_all.at[:, pl.ds(al((1 - c) * comp, 128), comp)], "q", 0)
    live_text = lax.broadcasted_iota(jnp.int32, (text_pad, 2 * comp), 0) < txt
    numer, denom = [], []
    for h in range(heads_half):
        hs = slice(h * HEAD, (h + 1) * HEAD)
        keys = head_norm(text_k[hs], gain_ref[:, 2:3]).T.astype(bf16)
        scores = jnp.dot(keys, q_all[hs, :], preferred_element_type=f32)
        weights_t = jnp.where(live_text, jnp.exp(scores), 0.0)
        denom.append(jnp.sum(weights_t, axis=0, keepdims=True))
        numer.append(jnp.dot(text_v[hs], weights_t.astype(bf16), preferred_element_type=f32))
    for o in range(1, group):
        pos = lax.rem(gpos + o, group)
        arrived(kv_all.at[:, :, pl.ds(al(pos * comp, 128), comp)], "kv", pos)
    for h in range(heads_half):
        hs = slice(h * HEAD, (h + 1) * HEAD)
        keys = kv_all[0, hs, :].astype(f32).T.astype(bf16)
        weights_t = jnp.exp(jnp.dot(keys, q_all[hs, :], preferred_element_type=f32))
        total = denom[h] + jnp.sum(weights_t, axis=0, keepdims=True)
        mixed = numer[h] + jnp.dot(
            kv_all[1, hs, :], weights_t.astype(bf16), preferred_element_type=f32
        )
        attended = (mixed / total).astype(bf16)
        att_snd[0, hs, :] = attended[:, :comp]
        att_snd[1, hs, :] = attended[:, comp:]
    push(att_snd.at[1 - c], att_t.at[pl.ds(al(c * hcols, 16), hcols), :], "d", 0, (sib, m))
    att_t[pl.ds(al(c * hcols, 16), hcols), :] = att_snd[c]
    loads[1].wait()
    arrived(att_t.at[pl.ds(al((1 - c) * hcols, 16), hcols), :], "d", 0)

    def reduce_over_mlp(lhs, w_ref, gate_row, buf, recv, name):
        sent = 0
        for start, size in column_chunks(width, 256):
            block = jnp.dot(lhs, w_ref[:, start:start + size], preferred_element_type=f32)
            block = block * mod_ref[gate_row:gate_row + 1, start:start + size]
            buf[start:start + size, :] = block.T.astype(bf16)
            while sent < nz and (sent + 1) * share <= start + size:
                send_to(buf, recv, name, sent)
                sent += 1
        for o in range(1, nz):
            z = lax.rem(m + o, nz)
            arrived(recv.at[z], name, z)
        total = buf[pl.ds(al(m * share, 16), share), :].astype(f32)
        for o in range(1, nz):
            total = total + recv[lax.rem(m + o, nz)].astype(f32)
        return total

    waits = []

    def send_to(buf, recv, name, z):
        index = counter[0]
        counter[0] += 1
        copy = pltpu.make_async_remote_copy(
            src_ref=buf.at[z * share:(z + 1) * share, :], dst_ref=recv.at[m],
            send_sem=send_sem.at[index], recv_sem=recv_sem.at[rbase[name] + m],
            device_id=(p, z), device_id_type=MESH,
        )

        @pl.when(m != z)
        def _():
            copy.start()

        waits.append((z, copy))

    attended = att_t[...].astype(f32).T.astype(bf16)
    ga = reduce_over_mlp(attended, wo, 2, part_t, recv_e, "e")
    ga_low = ga.astype(bf16)
    ga_rows = pl.ds(al(m * share, 16), share)
    ga_t[ga_rows, :] = ga_low
    for o in range(1, nz):
        push(ga_t.at[ga_rows, :], ga_t.at[ga_rows, :], "f", m, (p, lax.rem(m + o, nz)))
    loads[2].wait()
    for o in range(1, nz):
        z = lax.rem(m + o, nz)
        arrived(ga_t.at[pl.ds(al(z * share, 16), share), :], "f", z)
    after = x_all + ga_t[...].astype(f32).T
    normed_two = (layer_norm(after) * (1.0 + mod_ref[4:5, :]) + mod_ref[3:4, :]).astype(bf16)
    hidden = []
    for start, size in column_chunks(wu.shape[1], 256):
        up = jnp.dot(normed_two, wu[:, start:start + size], preferred_element_type=f32)
        hidden.append(jax.nn.gelu(up, approximate=True).astype(bf16))
    hidden = jnp.concatenate(hidden, axis=1)
    loads[3].wait()
    gm = reduce_over_mlp(hidden, wd, 5, mid_t, recv_g, "g")
    x_own = x_t[ga_rows, :].astype(f32)
    step = mod_ref[6:7, :comp]
    fin_t[...] = (x_own + step * (x_own + ga + gm)).astype(bf16)

    for o in range(1, n):
        d = lax.rem(p + o, n)
        push(
            fin_t.at[pl.ds(al(lax.rem(d, 2) * half, 16), half), :],
            recv_f.at[:, pl.ds(al(p * comp, 128), comp)], "h", p, (d, m),
        )
    recv_f[:, pl.ds(al(p * comp, 128), comp)] = fin_t[pl.ds(al(c * half, 16), half), :]
    for o in range(1, n):
        s = lax.rem(p + o, n)
        arrived(recv_f.at[:, pl.ds(al(s * comp, 128), comp)], "h", s)
    spread = jnp.dot(recv_f[...], e_ref[...], preferred_element_type=f32).astype(bf16)
    res[0] = spread[:, :cap]
    res[1] = spread[:, cap:]
    push(res.at[1 - c], recv_i, "i", 0, (sib, m))
    out_ref[pl.ds(al(c * half, 16), half), :] = res[c]
    arrived(recv_i, "i", 0)
    out_ref[pl.ds(al((1 - c) * half, 16), half), :] = recv_i[...]
    for copy in sends:
        copy.wait_send()
    for z, copy in waits:
        @pl.when(m != z)
        def _():
            copy.wait_send()


def body(
    n, nz,
    latent, split_list, modulation, w_qkv, w_out, w_up, w_down, qk_gains, text_kv, timestep, step_sizes,
):
    cap, share = latent.shape
    width = share * nz
    items = modulation.shape[0]
    comp = items * IMG // n
    group = IMG // comp
    cols = w_out.shape[0]
    hcols = cols // 2
    hidden = w_up.shape[1]
    txt = text_kv.shape[2]
    text_pad = -(-txt // 128) * 128
    half = share // 2

    item = lax.axis_index("patch") // group
    mods = lax.dynamic_index_in_dim(modulation, item, 0, keepdims=False)
    step = step_sizes[lax.dynamic_index_in_dim(timestep, item, 0, keepdims=False)]
    mods = jnp.concatenate([mods, jnp.broadcast_to(step, (2, width))], axis=0)
    split = jnp.broadcast_to(jnp.pad(split_list.astype(f32), ((0, 0), (0, 124))), (8, 128))
    gains = jnp.pad(qk_gains.T, ((0, 0), (0, 125)))
    text = lax.dynamic_index_in_dim(text_kv, item, 1, keepdims=False)
    text = jnp.pad(jnp.swapaxes(text, 1, 2), ((0, 0), (0, 0), (0, text_pad - txt)))

    vmem = pl.BlockSpec(memory_space=pltpu.VMEM)
    hbm = pl.BlockSpec(memory_space=pl.ANY)
    recv_count = 2 * n + 2 * nz + 1 + group + 1 + 3 * nz + n + 1
    send_count = 3 * (n - 1) + 2 * (nz - 1) + 1 + group - 1 + 1 + 1 + 2 * nz + nz - 1 + 1
    out = pl.pallas_call(
        functools.partial(kernel, n, nz, txt),
        out_shape=jax.ShapeDtypeStruct((share, cap), bf16),
        in_specs=[vmem] * 5 + [hbm] * 4,
        out_specs=vmem,
        scratch_shapes=[
            pltpu.VMEM((3, width, cols), bf16),
            pltpu.VMEM((cols, width), bf16),
            pltpu.VMEM((width, hidden), bf16),
            pltpu.VMEM((hidden, width), bf16),
            pltpu.VMEM((n * 8, 128), f32),
            pltpu.VMEM((n * 8, cap), f32),
            pltpu.VMEM((half, n * cap), bf16),
            pltpu.VMEM((2 * comp, n * cap), bf16),
            pltpu.VMEM((n * comp, 2 * cap), bf16),
            pltpu.VMEM((2, half, comp), bf16),
            pltpu.VMEM((width, comp), bf16),
            pltpu.VMEM((cols, comp), bf16),
            pltpu.VMEM((2, cols, comp), bf16),
            pltpu.VMEM((hcols, 2 * comp), bf16),
            pltpu.VMEM((2, hcols, group * comp), bf16),
            pltpu.VMEM((2, hcols, comp), bf16),
            pltpu.VMEM((cols, comp), bf16),
            pltpu.VMEM((width, comp), bf16),
            pltpu.VMEM((nz, share, comp), bf16),
            pltpu.VMEM((width, comp), bf16),
            pltpu.VMEM((width, comp), bf16),
            pltpu.VMEM((nz, share, comp), bf16),
            pltpu.VMEM((share, comp), bf16),
            pltpu.VMEM((half, n * comp), bf16),
            pltpu.VMEM((2, half, cap), bf16),
            pltpu.VMEM((half, cap), bf16),
            pltpu.SemaphoreType.DMA((4,)),
            pltpu.SemaphoreType.DMA((send_count,)),
            pltpu.SemaphoreType.DMA((recv_count,)),
        ],
        compiler_params=pltpu.CompilerParams(
            collective_id=0, has_side_effects=True, vmem_limit_bytes=58 * 1024 * 1024
        ),
    )(latent.T, split, mods, gains, text, jnp.swapaxes(w_qkv, 0, 1), w_out, w_up, w_down)
    return out.T


def solution(mesh):
    return jax.shard_map(
        functools.partial(body, mesh.shape["patch"], mesh.shape["mlp"]),
        mesh=mesh,
        in_specs=(
            P("patch", "mlp"),
            P("patch", None),
            P(),
            P(None, None, "mlp"),
            P("mlp", None),
            P(None, "mlp"),
            P("mlp", None),
            P(),
            P(None, None, None, "mlp"),
            P(),
            P(),
        ),
        out_specs=P("patch", "mlp"),
        check_vma=False,
    )
```

time: 321 us -> 119 us (0.37)
  waiting for transfers between devices: 166 us -> 0 us
  Pallas kernels: 0 us -> 107 us
  other arithmetic: 44.3 us -> 0.66 us
  local copies, waits for them, and re-layouts: 45.1 us -> 9.12 us
  matrix products: 32.5 us -> 0 us
  between operations: 18.6 us -> 0.68 us
  blocking collectives: 9.01 us -> 0 us
    pallas_call x0 -> x1, Pallas kernels: none -> 107 us  [body(): pl.pallas_call(functools.partial(kernel, n, nz, txt), out_shape=jax.Shape...]
    psum x1 -> x0, waiting for transfers between devices: 98 us -> none  [body(): attn_total = lax.psum(head_part, 'mlp')]
    unnamed x6 -> x0, waiting for transfers between devices: 46.6 us -> none
    all_gather x3 -> x0, waiting for transfers between devices: 21.7 us -> none  [the longest x1 21.7 us: body(): row_data = lax.all_gather(latent, 'mlp', axis=1, tiled=True)]
    dot_general x12 -> x0, matrix products: 20.5 us -> none  [the longest x5 8.96 us: attend_dense(): jnp.einsum('qhd,khd->qhk', query_heads, key_heads, preferred_element_type...]
    convert_element_type x13 -> x1, other arithmetic: 16.1 us -> 0.66 us  [body(): split_list.astype(f32)]
    unnamed x1 -> x0, matrix products: 12 us -> none
    mul x16 -> x0, local copies, waits for them, and re-layouts: 10 us -> none  [the longest x13 5.09 us: head_norm(): shaped * lax.rsqrt(mean_square + norm_eps) * gain_row]
  transfers between devices with their start and end apart: 5 -> 0, of which waited for: 3 -> 0; matrix products, arithmetic and copies ran while one was open for 18% -> 0% of each run, Pallas kernels for 0% -> 0%
where the time goes in v1:
time: 119 us; the launch traced here: 117 us
  Pallas kernels  107 us (90%)
  local copies, waits for them, and re-layouts  9.12 us (8%)
    pallas_call x1, Pallas kernels, body(): pl.pallas_call(functools.partial(kernel, n, nz, txt), out_shape=jax.Shape...  107 us
    unnamed x4, local copies, waits for them, and re-layouts  4.45 us

profile of v1, /device:TPU:0, one launch (start us, length us, event | category | flops | bytes accessed | tf_op | source)
XLA Modules:
  0.0 117.1 jit_solution(5598324082747863436)
XLA Ops:
  0.7 1.3 %dynamic_slice.9 = f32[1]{0:T(128)} dynamic-slice(f32[28]{0:T(128)} %param.21, s32[]{:T(128)S(6)} %select_n.12), dynamic_slice_sizes={1} | dynamic-slice | bytes 12 | tf_op jit(solution)/shard_map/dynamic_slice | solution.py:334
  2.0 0.8 copy.16
  2.8 1.3 %concatenate.3.mod_ref = f32[8,2432]{1,0:T(8,128)} pad(f32[6,2432]{1,0:T(8,128)S(1)} %bitcast.20, f32[]{:T(128)} %bitcast.3), padding=0_2x0_0 | pad | bytes 136196 | tf_op jit(solution)/shard_map/concatenate | solution.py:335
  4.1 1.1 copy.13
  5.3 0.8 pad.15.text_ref
  6.1 0.8 copy.12
  6.9 0.6 pad.14.gain_ref
  7.5 0.7 convert_element_type.9
  8.1 0.6 broadcast_in_dim.9.split_ref
  8.7 106.7 %shard_map.109 = bf16[608,256]{1,0:T(8,128)(2,1)} custom-call(bf16[608,256]{1,0:T(8,128)(2,1)} %bitcast.21, f32[8,128]{1,0:T(8,128)} %broadcast_in_dim.9.split_ref, f32[8,2432]{1,0:T(8,128)} %concatenate.3.mod_ref, f32[64,128]{1,0:T(8,128)} %pad.14.gain_ref, bf16[2,384,256]{2,1,0:T(8,128)(2,1)} %pad.15.text_ref, bf16[3,2432,384]{2,1,0:T(8,128)(2,1)} %bitcast.17, ...), custom_call_target="tpu_custom_call" | custom-call | tf_op jit(solution)/shard_map/pallas_call | solution.py:345
  115.4 1.7 %copy.19 = bf16[256,608]{0,1:T(8,128)(2,1)} copy(bf16[256,608]{0,1:T(8,128)(2,1)} %bitcast.19) | data formatting | bytes 622592
  (1 shorter events, 0.0 us)

commit v2 on v1

--- a/solution.py
+++ b/solution.py
@@ -37,10 +37,10 @@
 
 def kernel(
     n, nz, txt,
-    lat_ref, split_ref, mod_ref, gain_ref, text_ref, wq_hbm, wo_hbm, wu_hbm, wd_hbm,
+    lat_ref, list_ref, mods_ref, gains_ref, texts_ref, time_ref, steps_ref, wq_hbm, wo_hbm, wu_hbm, wd_hbm,
     out_ref,
-    wq, wo, wu, wd, split_all, t_ref, recv_a, m_ref, e_ref, sel, x_t, q_t, kv_t, q_all, kv_all,
-    att_snd, att_t, part_t, recv_e, ga_t, mid_t, recv_g, fin_t, recv_f, res, recv_i,
+    wq, wo, wu, wd, split_ref, gain_pad, text_rows, text_t, split_all, t_ref, recv_a, m_ref, e_ref, sel, x_t, q_t, kv_t, q_all, kv_all,
+    att_snd, att_t, part_t, recv_e, ga_t, ga_own, mid_t, recv_g, fin_t, recv_f, res, recv_i,
     w_sem, send_sem, recv_sem,
 ):
     p = lax.axis_index("patch")
@@ -67,6 +67,17 @@
     for load in loads:
         load.start()
 
+    item = p // group
+    lane8 = lax.broadcasted_iota(jnp.int32, (8, 128), 1)
+    listed = jnp.zeros((8, 128), jnp.int32)
+    for k in range(4):
+        listed = jnp.where(lane8 == k, list_ref[0, k], listed)
+    split_ref[...] = listed.astype(f32)
+    step = steps_ref[time_ref[item]]
+
+    def mod(row):
+        return mods_ref[item, row:row + 1, :]
+
     barrier = pltpu.get_barrier_semaphore()
     for o in range(1, n):
         pl.semaphore_signal(barrier, inc=1, device_id=(lax.rem(p + o, n), m), device_id_type=MESH)
@@ -80,8 +91,8 @@
     rbase = {}
     spot = 0
     for name, count in (
-        ("split", n), ("a", n), ("b", 2 * nz), ("q", 1), ("kv", group), ("d", 1),
-        ("e", nz), ("f", nz), ("g", nz), ("h", n), ("i", 1),
+        ("split", n), ("a", 2 * n), ("b", 4 * nz), ("q", 1), ("kv", group), ("d", 1),
+        ("e", 2 * nz), ("f", 2 * nz), ("g", 2 * nz), ("h", n), ("i", 1),
     ):
         rbase[name] = spot
         spot += count
@@ -104,12 +115,15 @@
     for o in range(1, n):
         d = lax.rem(p + o, n)
         push(split_ref, split_all.at[pl.ds(al(p * 8, 8), 8), :], "split", p, (d, m))
-    for o in range(1, n):
-        d = lax.rem(p + o, n)
-        push(
-            lat_ref.at[pl.ds(al(lax.rem(d, 2) * half, 16), half), :],
-            recv_a.at[:, pl.ds(al(p * cap, 128), cap)], "a", p, (d, m),
-        )
+    first = -(-half // 32) * 16
+    parts = ((0, first), (first, half - first))
+    for k, (start, size) in enumerate(parts):
+        for o in range(1, n):
+            d = lax.rem(p + o, n)
+            push(
+                lat_ref.at[pl.ds(al(lax.rem(d, 2) * half + start, 16), size), :],
+                recv_a.at[start:start + size, pl.ds(al(p * cap, 128), cap)], "a", 2 * p + k, (d, m),
+            )
     split_all[pl.ds(al(p * 8, 8), 8), :] = split_ref[...]
     recv_a[:, pl.ds(al(p * cap, 128), cap)] = lat_ref[pl.ds(al(c * half, 16), half), :]
     for o in range(1, n):
@@ -147,31 +161,43 @@
             e_ref[s * comp:(s + 1) * comp, k * cap:(k + 1) * cap] = jnp.where(
                 mine == rows, 1.0, 0.0
             ).astype(bf16)
-    for o in range(1, n):
-        s = lax.rem(p + o, n)
-        arrived(recv_a.at[:, pl.ds(al(s * cap, 128), cap)], "a", s)
-    chosen = lax.dot_general(
-        recv_a[...], m_ref[...], (((1,), (1,)), ((), ())), preferred_element_type=f32
-    ).astype(bf16)
-    sel[0] = chosen[:, :comp]
-    sel[1] = chosen[:, comp:]
-
-    def x_rows(z, core):
-        return pl.ds(al(z * share + core * half, 16), half)
-
-    for o in range(1, nz):
-        z = lax.rem(m + o, nz)
-        for k in range(2):
-            push(sel.at[k], x_t.at[x_rows(m, c), :], "b", 2 * m + c, (2 * pair + k, z))
-    push(sel.at[1 - c], x_t.at[x_rows(m, c), :], "b", 2 * m + c, (sib, m))
-    x_t[x_rows(m, c), :] = sel[c]
-    arrived(x_t.at[x_rows(m, 1 - c), :], "b", 2 * m + 1 - c)
-    for o in range(1, nz):
-        z = lax.rem(m + o, nz)
-        for k in range(2):
-            arrived(x_t.at[x_rows(z, k), :], "b", 2 * z + k)
+    gain_pad[...] = jnp.zeros_like(gain_pad)
+    gain_pad[0:gains_ref.shape[0], 0:HEAD] = gains_ref[...]
+    gain_ref = gain_pad[...].T[:HEAD, :]
+    text_rows[...] = jnp.zeros_like(text_rows)
+    for k in range(2):
+        text_rows[0:txt, :] = texts_ref[k, item].astype(f32)
+        text_t[k] = text_rows[...].T.astype(bf16)
+
+    def x_rows(z, core, part):
+        return pl.ds(al(z * share + core * half + part[0], 16), part[1])
+
+    for k, (start, size) in enumerate(parts):
+        for o in range(1, n):
+            s = lax.rem(p + o, n)
+            arrived(recv_a.at[start:start + size, pl.ds(al(s * cap, 128), cap)], "a", 2 * s + k)
+        chosen = lax.dot_general(
+            recv_a[start:start + size, :], m_ref[...], (((1,), (1,)), ((), ())),
+            preferred_element_type=f32,
+        ).astype(bf16)
+        sel[0, start:start + size, :] = chosen[:, :comp]
+        sel[1, start:start + size, :] = chosen[:, comp:]
+        mine = x_rows(m, c, (start, size))
+        spot_b = 2 * (2 * m + c) + k
+        for o in range(1, nz):
+            z = lax.rem(m + o, nz)
+            for q in range(2):
+                push(sel.at[q, start:start + size, :], x_t.at[mine, :], "b", spot_b, (2 * pair + q, z))
+        push(sel.at[1 - c, start:start + size, :], x_t.at[mine, :], "b", spot_b, (sib, m))
+        x_t[mine, :] = sel[c, start:start + size, :]
+    for k, part in enumerate(parts):
+        arrived(x_t.at[x_rows(m, 1 - c, part), :], "b", 2 * (2 * m + 1 - c) + k)
+        for o in range(1, nz):
+            z = lax.rem(m + o, nz)
+            for q in range(2):
+                arrived(x_t.at[x_rows(z, q, part), :], "b", 2 * (2 * z + q) + k)
     x_all = x_t[...].astype(f32).T
-    normed = (layer_norm(x_all) * (1.0 + mod_ref[1:2, :]) + mod_ref[0:1, :]).astype(bf16)
+    normed = (layer_norm(x_all) * (1.0 + mod(1)) + mod(0)).astype(bf16)
     loads[0].wait()
     for j, (gain_col, scale) in enumerate(((1, 1.0), (None, 1.0), (0, HEAD ** -0.5))):
         which = (1, 2, 0)[j]
@@ -198,9 +224,9 @@
     )
     q_all[:, pl.ds(al(c * comp, 128), comp)] = q_t[pl.ds(al(c * hcols, 16), hcols), :]
 
-    text_pad = text_ref.shape[2]
-    text_k = text_ref[0, pl.ds(al(c * hcols, 16), hcols), :].astype(f32)
-    text_v = text_ref[1, pl.ds(al(c * hcols, 16), hcols), :]
+    text_pad = text_t.shape[2]
+    text_k = text_t[0, pl.ds(al(c * hcols, 16), hcols), :].astype(f32)
+    text_v = text_t[1, pl.ds(al(c * hcols, 16), hcols), :]
     arrived(q_all.at[:, pl.ds(al((1 - c) * comp, 128), comp)], "q", 0)
     live_text = lax.broadcasted_iota(jnp.int32, (text_pad, 2 * comp), 0) < txt
     numer, denom = [], []
@@ -230,70 +256,117 @@
     loads[1].wait()
     arrived(att_t.at[pl.ds(al((1 - c) * hcols, 16), hcols), :], "d", 0)
 
-    def reduce_over_mlp(lhs, w_ref, gate_row, buf, recv, name):
+    halves = ((0, half), (half, share - half))
+    line_sends = []
+
+    def scatter_over_mlp(lhs, w_ref, gate_row, buf, recv, name, early):
         sent = 0
         for start, size in column_chunks(width, 256):
             block = jnp.dot(lhs, w_ref[:, start:start + size], preferred_element_type=f32)
-            block = block * mod_ref[gate_row:gate_row + 1, start:start + size]
+            block = block * mods_ref[item, gate_row:gate_row + 1, start:start + size]
             buf[start:start + size, :] = block.T.astype(bf16)
-            while sent < nz and (sent + 1) * share <= start + size:
-                send_to(buf, recv, name, sent)
+            while early and sent < nz and (sent + 1) * share <= start + size:
+                for k, part in enumerate(halves):
+                    index = counter[0]
+                    counter[0] += 1
+                    copy = pltpu.make_async_remote_copy(
+                        src_ref=buf.at[sent * share + part[0]:sent * share + part[0] + part[1], :],
+                        dst_ref=recv.at[m, part[0]:part[0] + part[1], :],
+                        send_sem=send_sem.at[index], recv_sem=recv_sem.at[rbase[name] + 2 * m + k],
+                        device_id=(p, sent), device_id_type=MESH,
+                    )
+
+                    @pl.when(m != sent)
+                    def _():
+                        copy.start()
+                    line_sends.append((m != sent, copy))
                 sent += 1
+        if not early:
+            for k, part in enumerate(halves):
+                for o in range(1, nz):
+                    z = lax.rem(m + o, nz)
+                    push(
+                        buf.at[pl.ds(al(z * share + part[0], 16), part[1]), :],
+                        recv.at[m, part[0]:part[0] + part[1], :], name, 2 * m + k, (p, z),
+                    )
+
+    def summed(buf, recv, name, k):
+        start, size = halves[k]
         for o in range(1, nz):
             z = lax.rem(m + o, nz)
-            arrived(recv.at[z], name, z)
-        total = buf[pl.ds(al(m * share, 16), share), :].astype(f32)
+            arrived(recv.at[z, start:start + size, :], name, 2 * z + k)
+        total = buf[pl.ds(al(m * share + start, 16), size), :].astype(f32)
         for o in range(1, nz):
-            total = total + recv[lax.rem(m + o, nz)].astype(f32)
+            total = total + recv[lax.rem(m + o, nz), start:start + size, :].astype(f32)
         return total
 
-    waits = []
-
-    def send_to(buf, recv, name, z):
-        index = counter[0]
-        counter[0] += 1
-        copy = pltpu.make_async_remote_copy(
-            src_ref=buf.at[z * share:(z + 1) * share, :], dst_ref=recv.at[m],
-            send_sem=send_sem.at[index], recv_sem=recv_sem.at[rbase[name] + m],
-            device_id=(p, z), device_id_type=MESH,
-        )
-
-        @pl.when(m != z)
-        def _():
-            copy.start()
-
-        waits.append((z, copy))
+    def line_hop(buf, name, s, k):
+        start, size = halves[k]
+        for way in (1, -1):
+            block = m - way * s
+            held_here = (block >= 0) & (block < nz)
+            safe = lax.rem(block + nz, nz)
+            index = counter[0]
+            counter[0] += 1
+            ref = buf.at[pl.ds(al(safe * share + start, 16), size), :]
+            copy = pltpu.make_async_remote_copy(
+                src_ref=ref, dst_ref=ref, send_sem=send_sem.at[index],
+                recv_sem=recv_sem.at[rbase[name] + 2 * safe + k],
+                device_id=(p, lax.rem(m + way + nz, nz)), device_id_type=MESH,
+            )
+            if s > 0:
+                @pl.when(held_here)
+                def _():
+                    copy.wait_recv()
+            if s < nz - 1:
+                go = held_here & (m + way >= 0) & (m + way < nz)
+
+                @pl.when(go)
+                def _():
+                    copy.start()
+                line_sends.append((go, copy))
 
     attended = att_t[...].astype(f32).T.astype(bf16)
-    ga = reduce_over_mlp(attended, wo, 2, part_t, recv_e, "e")
-    ga_low = ga.astype(bf16)
-    ga_rows = pl.ds(al(m * share, 16), share)
-    ga_t[ga_rows, :] = ga_low
-    for o in range(1, nz):
-        push(ga_t.at[ga_rows, :], ga_t.at[ga_rows, :], "f", m, (p, lax.rem(m + o, nz)))
+    scatter_over_mlp(attended, wo, 2, part_t, recv_e, "e", False)
+    own_rows = [pl.ds(al(m * share + start, 16), size) for start, size in halves]
+    for k in range(2):
+        ga = summed(part_t, recv_e, "e", k)
+        ga_own[halves[k][0]:halves[k][0] + halves[k][1], :] = ga
+        ga_t[own_rows[k], :] = ga.astype(bf16)
+        line_hop(ga_t, "f", 0, k)
     loads[2].wait()
-    for o in range(1, nz):
-        z = lax.rem(m + o, nz)
-        arrived(ga_t.at[pl.ds(al(z * share, 16), share), :], "f", z)
+    for s in range(1, nz):
+        for k in range(2):
+            line_hop(ga_t, "f", s, k)
     after = x_all + ga_t[...].astype(f32).T
-    normed_two = (layer_norm(after) * (1.0 + mod_ref[4:5, :]) + mod_ref[3:4, :]).astype(bf16)
+    normed_two = (layer_norm(after) * (1.0 + mod(4)) + mod(3)).astype(bf16)
     hidden = []
     for start, size in column_chunks(wu.shape[1], 256):
         up = jnp.dot(normed_two, wu[:, start:start + size], preferred_element_type=f32)
         hidden.append(jax.nn.gelu(up, approximate=True).astype(bf16))
     hidden = jnp.concatenate(hidden, axis=1)
     loads[3].wait()
-    gm = reduce_over_mlp(hidden, wd, 5, mid_t, recv_g, "g")
-    x_own = x_t[ga_rows, :].astype(f32)
-    step = mod_ref[6:7, :comp]
-    fin_t[...] = (x_own + step * (x_own + ga + gm)).astype(bf16)
-
-    for o in range(1, n):
-        d = lax.rem(p + o, n)
-        push(
-            fin_t.at[pl.ds(al(lax.rem(d, 2) * half, 16), half), :],
-            recv_f.at[:, pl.ds(al(p * comp, 128), comp)], "h", p, (d, m),
-        )
+    scatter_over_mlp(hidden, wd, 5, mid_t, recv_g, "g", True)
+
+    for k in range(2):
+        gm = summed(mid_t, recv_g, "g", k)
+        own = slice(halves[k][0], halves[k][0] + halves[k][1])
+        x_own = x_t[own_rows[k], :].astype(f32)
+        fin_t[own, :] = (x_own + step * (x_own + ga_own[own, :] + gm)).astype(bf16)
+        for o in range(0, n, 2):
+            d = lax.rem(pair * 2 + k + o, n)
+            index = counter[0]
+            counter[0] += 1
+            copy = pltpu.make_async_remote_copy(
+                src_ref=fin_t.at[own, :], dst_ref=recv_f.at[:, pl.ds(al(p * comp, 128), comp)],
+                send_sem=send_sem.at[index], recv_sem=recv_sem.at[rbase["h"] + p],
+                device_id=(d, m), device_id_type=MESH,
+            )
+
+            @pl.when(d != p)
+            def _():
+                copy.start()
+            line_sends.append((d != p, copy))
     recv_f[:, pl.ds(al(p * comp, 128), comp)] = fin_t[pl.ds(al(c * half, 16), half), :]
     for o in range(1, n):
         s = lax.rem(p + o, n)
@@ -307,8 +380,8 @@
     out_ref[pl.ds(al((1 - c) * half, 16), half), :] = recv_i[...]
     for copy in sends:
         copy.wait_send()
-    for z, copy in waits:
-        @pl.when(m != z)
+    for go, copy in line_sends:
+        @pl.when(go)
         def _():
             copy.wait_send()
 
@@ -329,29 +402,25 @@
     text_pad = -(-txt // 128) * 128
     half = share // 2
 
-    item = lax.axis_index("patch") // group
-    mods = lax.dynamic_index_in_dim(modulation, item, 0, keepdims=False)
-    step = step_sizes[lax.dynamic_index_in_dim(timestep, item, 0, keepdims=False)]
-    mods = jnp.concatenate([mods, jnp.broadcast_to(step, (2, width))], axis=0)
-    split = jnp.broadcast_to(jnp.pad(split_list.astype(f32), ((0, 0), (0, 124))), (8, 128))
-    gains = jnp.pad(qk_gains.T, ((0, 0), (0, 125)))
-    text = lax.dynamic_index_in_dim(text_kv, item, 1, keepdims=False)
-    text = jnp.pad(jnp.swapaxes(text, 1, 2), ((0, 0), (0, 0), (0, text_pad - txt)))
-
     vmem = pl.BlockSpec(memory_space=pltpu.VMEM)
+    smem = pl.BlockSpec(memory_space=pltpu.SMEM)
     hbm = pl.BlockSpec(memory_space=pl.ANY)
-    recv_count = 2 * n + 2 * nz + 1 + group + 1 + 3 * nz + n + 1
-    send_count = 3 * (n - 1) + 2 * (nz - 1) + 1 + group - 1 + 1 + 1 + 2 * nz + nz - 1 + 1
+    recv_count = 4 * n + 10 * nz + group + 3
+    send_count = 4 * n + 4 * nz + group + 16 * nz + n + 4
     out = pl.pallas_call(
         functools.partial(kernel, n, nz, txt),
         out_shape=jax.ShapeDtypeStruct((share, cap), bf16),
-        in_specs=[vmem] * 5 + [hbm] * 4,
+        in_specs=[vmem, smem, vmem, vmem, vmem, smem, smem] + [hbm] * 4,
         out_specs=vmem,
         scratch_shapes=[
             pltpu.VMEM((3, width, cols), bf16),
             pltpu.VMEM((cols, width), bf16),
             pltpu.VMEM((width, hidden), bf16),
             pltpu.VMEM((hidden, width), bf16),
+            pltpu.VMEM((8, 128), f32),
+            pltpu.VMEM((128, 128), f32),
+            pltpu.VMEM((text_pad, cols), f32),
+            pltpu.VMEM((2, cols, text_pad), bf16),
             pltpu.VMEM((n * 8, 128), f32),
             pltpu.VMEM((n * 8, cap), f32),
             pltpu.VMEM((half, n * cap), bf16),
@@ -368,6 +437,7 @@
             pltpu.VMEM((width, comp), bf16),
             pltpu.VMEM((nz, share, comp), bf16),
             pltpu.VMEM((width, comp), bf16),
+            pltpu.VMEM((share, comp), f32),
             pltpu.VMEM((width, comp), bf16),
             pltpu.VMEM((nz, share, comp), bf16),
             pltpu.VMEM((share, comp), bf16),
@@ -381,7 +451,7 @@
         compiler_params=pltpu.CompilerParams(
             collective_id=0, has_side_effects=True, vmem_limit_bytes=58 * 1024 * 1024
         ),
-    )(latent.T, split, mods, gains, text, jnp.swapaxes(w_qkv, 0, 1), w_out, w_up, w_down)
+    )(latent.T, split_list, modulation, qk_gains, text_kv, timestep, step_sizes, jnp.swapaxes(w_qkv, 0, 1), w_out, w_up, w_down)
     return out.T
 
 

time: 119 us -> 101 us (0.85)
  the two profiles are of different devices: /device:TPU:0 before, /device:TPU:25 now
where the time goes in v2:
time: 101 us
  Pallas kernels  95 us (94%)
  local copies, waits for them, and re-layouts  4.85 us (5%)
    pallas_call x1, Pallas kernels, body(): pl.pallas_call(functools.partial(kernel, n, nz, txt), out_shape=jax.Shape...  95 us
    unnamed x3, local copies, waits for them, and re-layouts  4.85 us

profile of v2, /device:TPU:25, one launch (start us, length us, event | category | flops | bytes accessed | tf_op | source)
XLA Modules:
  0.0 100.5 jit_solution(17833481425571724013)
XLA Ops:
  0.7 1.5 %copy.12.mods_ref = f32[1,6,2432]{2,1,0:T(8,128)} copy(f32[1,6,2432]{2,0,1:T(1,128)} %param.13) | data formatting | bytes 116736 | tf_op args[2]
  2.1 1.7 %copy.13.texts_ref = bf16[2,1,154,384]{3,2,1,0:T(8,128)(2,1)} copy(bf16[2,1,154,384]{3,0,2,1:T(2,128)(2,1)} %param.19) | data formatting | bytes 473088 | tf_op args[8]
  3.8 95.0 %shard_map.109 = bf16[608,256]{1,0:T(8,128)(2,1)} custom-call(bf16[608,256]{1,0:T(8,128)(2,1)} %bitcast.5, s32[1,4]{1,0:T(1,128)} %list_ref.1, f32[1,6,2432]{2,1,0:T(8,128)} %copy.12.mods_ref, f32[3,64]{1,0:T(4,128)} %gains_ref.1, bf16[2,1,154,384]{3,2,1,0:T(8,128)(2,1)} %copy.13.texts_ref, s32[1]{0:T(128)S(6)} %copy.15.time_ref, f32[28]{0:T(128)} %steps_ref.1, ...), custom_call_target="tpu_custom_call" | custom-call | tf_op jit(solution)/shard_map/pallas_call | solution.py:410
  98.8 1.7 %copy.16 = bf16[256,608]{0,1:T(8,128)(2,1)} copy(bf16[256,608]{0,1:T(8,128)(2,1)} %bitcast.4) | data formatting | bytes 622592

commit v3 on v2

--- a/solution.py
+++ b/solution.py
@@ -76,7 +76,7 @@
     step = steps_ref[time_ref[item]]
 
     def mod(row):
-        return mods_ref[item, row:row + 1, :]
+        return mods_ref[row, item, :, :]
 
     barrier = pltpu.get_barrier_semaphore()
     for o in range(1, n):
@@ -91,7 +91,7 @@
     rbase = {}
     spot = 0
     for name, count in (
-        ("split", n), ("a", 2 * n), ("b", 4 * nz), ("q", 1), ("kv", group), ("d", 1),
+        ("split", n), ("a", 2 * n), ("b", 4 * nz), ("q", 1), ("kv", 2 * group), ("d", 1),
         ("e", 2 * nz), ("f", 2 * nz), ("g", 2 * nz), ("h", n), ("i", 1),
     ):
         rbase[name] = spot
@@ -166,7 +166,7 @@
     gain_ref = gain_pad[...].T[:HEAD, :]
     text_rows[...] = jnp.zeros_like(text_rows)
     for k in range(2):
-        text_rows[0:txt, :] = texts_ref[k, item].astype(f32)
+        text_rows[0:txt, :] = texts_ref[item].astype(f32)[:, k, :]
         text_t[k] = text_rows[...].T.astype(bf16)
 
     def x_rows(z, core, part):
@@ -210,14 +210,17 @@
                 q_t[h * HEAD:(h + 1) * HEAD, :] = rows.astype(bf16)
             else:
                 kv_t[which - 1, h * HEAD:(h + 1) * HEAD, :] = rows.astype(bf16)
-        if which == 2:
+        if which > 0:
             for o in range(1, group):
                 pos = lax.rem(gpos + o, group)
                 push(
-                    kv_t.at[:, pl.ds(al(lax.rem(pos, 2) * hcols, 16), hcols), :],
-                    kv_all.at[:, :, pl.ds(al(gpos * comp, 128), comp)], "kv", gpos, (gbase + pos, m),
+                    kv_t.at[which - 1, pl.ds(al(lax.rem(pos, 2) * hcols, 16), hcols), :],
+                    kv_all.at[which - 1, :, pl.ds(al(gpos * comp, 128), comp)],
+                    "kv", 2 * gpos + which - 1, (gbase + pos, m),
                 )
-            kv_all[:, :, pl.ds(al(gpos * comp, 128), comp)] = kv_t[:, pl.ds(al(c * hcols, 16), hcols), :]
+            kv_all[which - 1, :, pl.ds(al(gpos * comp, 128), comp)] = kv_t[
+                which - 1, pl.ds(al(c * hcols, 16), hcols), :
+            ]
     push(
         q_t.at[pl.ds(al((1 - c) * hcols, 16), hcols), :],
         q_all.at[:, pl.ds(al(c * comp, 128), comp)], "q", 0, (sib, m),
@@ -237,18 +240,24 @@
         weights_t = jnp.where(live_text, jnp.exp(scores), 0.0)
         denom.append(jnp.sum(weights_t, axis=0, keepdims=True))
         numer.append(jnp.dot(text_v[hs], weights_t.astype(bf16), preferred_element_type=f32))
-    for o in range(1, group):
-        pos = lax.rem(gpos + o, group)
-        arrived(kv_all.at[:, :, pl.ds(al(pos * comp, 128), comp)], "kv", pos)
+    def kv_arrived(k):
+        for o in range(1, group):
+            pos = lax.rem(gpos + o, group)
+            arrived(kv_all.at[k, :, pl.ds(al(pos * comp, 128), comp)], "kv", 2 * pos + k)
+
+    kv_arrived(0)
+    low = []
     for h in range(heads_half):
         hs = slice(h * HEAD, (h + 1) * HEAD)
         keys = kv_all[0, hs, :].astype(f32).T.astype(bf16)
         weights_t = jnp.exp(jnp.dot(keys, q_all[hs, :], preferred_element_type=f32))
-        total = denom[h] + jnp.sum(weights_t, axis=0, keepdims=True)
-        mixed = numer[h] + jnp.dot(
-            kv_all[1, hs, :], weights_t.astype(bf16), preferred_element_type=f32
-        )
-        attended = (mixed / total).astype(bf16)
+        denom[h] = denom[h] + jnp.sum(weights_t, axis=0, keepdims=True)
+        low.append(weights_t.astype(bf16))
+    kv_arrived(1)
+    for h in range(heads_half):
+        hs = slice(h * HEAD, (h + 1) * HEAD)
+        mixed = numer[h] + jnp.dot(kv_all[1, hs, :], low[h], preferred_element_type=f32)
+        attended = (mixed / denom[h]).astype(bf16)
         att_snd[0, hs, :] = attended[:, :comp]
         att_snd[1, hs, :] = attended[:, comp:]
     push(att_snd.at[1 - c], att_t.at[pl.ds(al(c * hcols, 16), hcols), :], "d", 0, (sib, m))
@@ -263,7 +272,7 @@
         sent = 0
         for start, size in column_chunks(width, 256):
             block = jnp.dot(lhs, w_ref[:, start:start + size], preferred_element_type=f32)
-            block = block * mods_ref[item, gate_row:gate_row + 1, start:start + size]
+            block = block * mods_ref[gate_row, item, :, start:start + size]
             buf[start:start + size, :] = block.T.astype(bf16)
             while early and sent < nz and (sent + 1) * share <= start + size:
                 for k, part in enumerate(halves):
@@ -346,7 +355,7 @@
         hidden.append(jax.nn.gelu(up, approximate=True).astype(bf16))
     hidden = jnp.concatenate(hidden, axis=1)
     loads[3].wait()
-    scatter_over_mlp(hidden, wd, 5, mid_t, recv_g, "g", True)
+    scatter_over_mlp(hidden, wd, 5, mid_t, recv_g, "g", False)
 
     for k in range(2):
         gm = summed(mid_t, recv_g, "g", k)
@@ -405,8 +414,8 @@
     vmem = pl.BlockSpec(memory_space=pltpu.VMEM)
     smem = pl.BlockSpec(memory_space=pltpu.SMEM)
     hbm = pl.BlockSpec(memory_space=pl.ANY)
-    recv_count = 4 * n + 10 * nz + group + 3
-    send_count = 4 * n + 4 * nz + group + 16 * nz + n + 4
+    recv_count = 4 * n + 10 * nz + 2 * group + 3
+    send_count = 4 * n + 4 * nz + 2 * group + 16 * nz + n + 4
     out = pl.pallas_call(
         functools.partial(kernel, n, nz, txt),
         out_shape=jax.ShapeDtypeStruct((share, cap), bf16),
@@ -451,7 +460,7 @@
         compiler_params=pltpu.CompilerParams(
             collective_id=0, has_side_effects=True, vmem_limit_bytes=58 * 1024 * 1024
         ),
-    )(latent.T, split_list, modulation, qk_gains, text_kv, timestep, step_sizes, jnp.swapaxes(w_qkv, 0, 1), w_out, w_up, w_down)
+    )(latent.T, split_list, jnp.swapaxes(modulation, 0, 1)[:, :, None, :], qk_gains, jnp.transpose(text_kv, (1, 2, 0, 3)), timestep, step_sizes, jnp.swapaxes(w_qkv, 0, 1), w_out, w_up, w_down)
     return out.T
 
 

time: 101 us -> 94.4 us (0.935)
  the two profiles are of different devices: /device:TPU:25 before, /device:TPU:0 now
where the time goes in v3:
time: 94.4 us; the launch traced here: 94.3 us
  Pallas kernels  91.9 us (97%)
  local copies, waits for them, and re-layouts  1.71 us (2%)
    pallas_call x1, Pallas kernels, body(): pl.pallas_call(functools.partial(kernel, n, nz, txt), out_shape=jax.Shape...  91.9 us

profile of v3, /device:TPU:0, one launch (start us, length us, event | category | flops | bytes accessed | tf_op | source)
XLA Modules:
  0.0 94.3 jit_solution(5780965802990781381)
XLA Ops:
  0.7 91.9 %shard_map.109 = bf16[608,256]{1,0:T(8,128)(2,1)} custom-call(bf16[608,256]{1,0:T(8,128)(2,1)} %bitcast.7, s32[1,4]{1,0:T(1,128)} %list_ref.1, f32[6,1,1,2432]{3,2,1,0:T(1,128)} %bitcast.9, f32[3,64]{1,0:T(4,128)} %gains_ref.1, bf16[1,154,2,384]{3,2,1,0:T(2,128)(2,1)} %bitcast.8, s32[1]{0:T(128)S(6)} %copy.13.time_ref, f32[28]{0:T(128)} %steps_ref.1, ...), custom_call_target="tpu_custom_call" | custom-call | tf_op jit(solution)/shard_map/pallas_call | solution.py:419
  92.6 1.7 %copy.14 = bf16[256,608]{0,1:T(8,128)(2,1)} copy(bf16[256,608]{0,1:T(8,128)(2,1)} %bitcast.6) | data formatting | bytes 622592
